TPU v7x, 1024 devices: a whole 4x8x16 slice. The times are simulated.
1024 devices in a mesh: blk: 16 (over z_hi, x, core), ulysses: 64 (over y, z_lo).
Axes of the slice: x: 4, y: 8, z: 16 (z_hi: 2, z_lo: 8; z = z_hi * 8 + z_lo), core: 2. Of those that a mesh axis runs over, the one named last changes fastest.
Arguments:
- query_rows: bfloat16 [32, 131072, 128], P(None, ('blk', 'ulysses')), may hold values from -160 to 160
- out_grad: bfloat16 [32, 131072, 128], P(None, ('blk', 'ulysses')), may hold values from -6 to 6
- key_rows: bfloat16 [32, 2048, 128], P(None, 'blk'), may hold values from -6 to 6
- value_rows: bfloat16 [32, 2048, 128], P(None, 'blk'), may hold values from -6 to 6
- routes: int32 [16, 16], replicated, may hold values from 0 to 7
Outputs:
- query_grad: bfloat16 [32, 131072, 128], P(None, ('blk', 'ulysses'))
- key_grad: float32 [32, 2048, 128], P(None, ('blk', 'ulysses'))
- value_grad: float32 [32, 2048, 128], P(None, ('blk', 'ulysses'))
All inputs are finite; a program needn't handle non-finite values.
Results may differ from a plain program's by a relative error of at most 0.0056.
Values may be sent and summed in bfloat16 or wider, within the bound.
A program may use at most 32 MiB of HBM per device.

v0:
```python
import math

import jax
import jax.numpy as jnp
from jax import lax
from jax.sharding import PartitionSpec as P

KB = 16


def body(query_rows, out_grad, key_rows, value_rows, routes):
    head_count, token_count, head_dim = query_rows.shape
    group_keys = key_rows.shape[1]
    cycle_size = lax.axis_size("blk")
    group_size = lax.axis_size("ulysses")
    sub_count = max(1, group_size // head_count)
    item_count = head_count * sub_count // group_size
    sub_length = token_count // sub_count
    row_count = group_size * sub_length
    block_count = group_keys // KB
    key_stride = token_count * group_size // group_keys
    score_scale = 1.0 / math.sqrt(head_dim)
    my_group = lax.axis_index("blk")
    my_rank = lax.axis_index("ulysses")
    packed_query = query_rows.reshape(head_count * sub_count, sub_length, head_dim)
    packed_grad = out_grad.reshape(head_count * sub_count, sub_length, head_dim)
    local_query, local_grad = (
        lax.all_to_all(packed_query, "ulysses", split_axis=0, concat_axis=1, tiled=True),
        lax.all_to_all(packed_grad, "ulysses", split_axis=0, concat_axis=1, tiled=True),
    )
    first_head = my_rank * item_count // sub_count
    own_keys = lax.dynamic_slice_in_dim(key_rows, first_head, item_count, 0)
    own_values = lax.dynamic_slice_in_dim(value_rows, first_head, item_count, 0)
    wanted = lax.dynamic_index_in_dim(routes, my_group, 0, keepdims=False)
    block_ids = jnp.arange(block_count, dtype=jnp.int32)
    whole_keys, whole_values = (
        lax.all_gather(own_keys, "blk", axis=1, tiled=True),
        lax.all_gather(own_values, "blk", axis=1, tiled=True),
    )
    picker = (wanted[:, None] == block_ids[None, :]).astype(jnp.bfloat16)
    shaped_keys = whole_keys.reshape(item_count, cycle_size, block_count, KB, head_dim)
    shaped_values = whole_values.reshape(item_count, cycle_size, block_count, KB, head_dim)
    far_keys = jnp.einsum(
        "jb,ijbkd->ijkd", picker, shaped_keys, preferred_element_type=jnp.float32
    ).astype(jnp.bfloat16)
    far_values = jnp.einsum(
        "jb,ijbkd->ijkd", picker, shaped_values, preferred_element_type=jnp.float32
    ).astype(jnp.bfloat16)
    near_keys = jnp.concatenate(
        [own_keys, far_keys.reshape(item_count, cycle_size * KB, head_dim)], axis=1
    )
    near_values = jnp.concatenate(
        [own_values, far_values.reshape(item_count, cycle_size * KB, head_dim)], axis=1
    )
    near_count = near_keys.shape[1]
    item_sub = (my_rank * item_count + jnp.arange(item_count, dtype=jnp.int32)) % sub_count
    far_visible = jnp.repeat(jnp.arange(cycle_size, dtype=jnp.int32) < my_group, KB)
    own_offsets = jnp.arange(group_keys, dtype=jnp.int32) * key_stride
    block_rows = 1024

    def attend(row_block, carried):
        query_out, key_acc, value_acc = carried
        row_start = row_block * block_rows
        queries = lax.dynamic_slice_in_dim(local_query, row_start, block_rows, 1)
        grad_rows = lax.dynamic_slice_in_dim(local_grad, row_start, block_rows, 1)
        row_ids = row_start + jnp.arange(block_rows, dtype=jnp.int32)
        positions = (
            row_ids[None, :] // sub_length * token_count
            + item_sub[:, None] * sub_length
            + row_ids[None, :] % sub_length
        )
        own_visible = own_offsets[None, None, :] <= positions[:, :, None]
        visible = jnp.concatenate(
            [
                own_visible,
                jnp.broadcast_to(far_visible, (item_count, block_rows, far_visible.shape[0])),
            ],
            axis=2,
        )
        scores = (
            jnp.einsum("ird,ikd->irk", queries, near_keys, preferred_element_type=jnp.float32)
            * score_scale
        )
        row_max = jnp.max(jnp.where(visible, scores, -jnp.inf), axis=-1, keepdims=True)
        expsum = jnp.where(visible, jnp.exp(scores - row_max), 0.0)
        weights = expsum / jnp.sum(expsum, axis=-1, keepdims=True)
        weights_half = weights.astype(jnp.bfloat16)
        attended = jnp.einsum(
            "irk,ikd->ird", weights_half, near_values, preferred_element_type=jnp.float32
        )
        delta_rows = jnp.sum(grad_rows.astype(jnp.float32) * attended, axis=-1, keepdims=True)
        dweights = jnp.einsum(
            "ird,ikd->irk", grad_rows, near_values, preferred_element_type=jnp.float32
        )
        dscore = (weights * (dweights - delta_rows)).astype(jnp.bfloat16)
        query_part = (
            jnp.einsum("irk,ikd->ird", dscore, near_keys, preferred_element_type=jnp.float32)
            * score_scale
        ).astype(jnp.bfloat16)
        key_acc = (
            key_acc
            + jnp.einsum("irk,ird->ikd", dscore, queries, preferred_element_type=jnp.float32)
            * score_scale
        )
        value_acc = value_acc + jnp.einsum(
            "irk,ird->ikd", weights_half, grad_rows, preferred_element_type=jnp.float32
        )
        query_out = lax.dynamic_update_slice_in_dim(query_out, query_part, row_start, 1)
        return (query_out, key_acc, value_acc)

    start_state = (
        jnp.zeros((item_count, row_count, head_dim), jnp.bfloat16),
        jnp.zeros((item_count, near_count, head_dim), jnp.float32),
        jnp.zeros((item_count, near_count, head_dim), jnp.float32),
    )
    query_out, key_acc, value_acc = lax.fori_loop(0, row_count // block_rows, attend, start_state)
    own_key_grad = key_acc[:, :group_keys]
    own_value_grad = value_acc[:, :group_keys]
    far_key_grad = key_acc[:, group_keys:].reshape(item_count, cycle_size, KB, head_dim)
    far_value_grad = value_acc[:, group_keys:].reshape(item_count, cycle_size, KB, head_dim)
    placer = (wanted[:, None] == block_ids[None, :]).astype(jnp.float32)
    spread_keys = (placer[None, :, :, None, None] * far_key_grad[:, :, None, :, :]).reshape(
        item_count, cycle_size * group_keys, head_dim
    )
    spread_values = (placer[None, :, :, None, None] * far_value_grad[:, :, None, :, :]).reshape(
        item_count, cycle_size * group_keys, head_dim
    )
    added_keys, added_values = (
        lax.psum_scatter(spread_keys, "blk", scatter_dimension=1, tiled=True),
        lax.psum_scatter(spread_values, "blk", scatter_dimension=1, tiled=True),
    )
    key_share = (own_key_grad + added_keys).astype(jnp.bfloat16)
    value_share = (own_value_grad + added_values).astype(jnp.bfloat16)
    query_back, key_back, value_back = (
        lax.all_to_all(query_out, "ulysses", split_axis=1, concat_axis=0, tiled=True),
        lax.all_to_all(key_share, "ulysses", split_axis=1, concat_axis=0, tiled=True),
        lax.all_to_all(value_share, "ulysses", split_axis=1, concat_axis=0, tiled=True),
    )
    query_grad = query_back.reshape(head_count, token_count, head_dim)
    key_grad = jnp.sum(
        key_back.astype(jnp.float32).reshape(head_count, sub_count, -1, head_dim), axis=1
    )
    value_grad = jnp.sum(
        value_back.astype(jnp.float32).reshape(head_count, sub_count, -1, head_dim), axis=1
    )
    return (query_grad, key_grad, value_grad)


def solution(mesh):
    return jax.shard_map(
        body,
        mesh=mesh,
        in_specs=(
            P(None, ("blk", "ulysses"), None),
            P(None, ("blk", "ulysses"), None),
            P(None, "blk", None),
            P(None, "blk", None),
            P(),
        ),
        out_specs=(
            P(None, ("blk", "ulysses"), None),
            P(None, ("blk", "ulysses"), None),
            P(None, ("blk", "ulysses"), None),
        ),
        check_vma=False,
    )
```

profile of v0, /device:TPU:2, one launch (start us, length us, event | category | flops | bytes accessed | tf_op | source)
XLA Modules:
  0.0 622.7 jit_solution(17097058894453609426)
XLA Ops:
  7.2 75.1 %all_to_all.51 = bf16[64,64,128]{2,1,0:T(8,128)(2,1)} all-to-all(bf16[64,64,128]{2,1,0:T(8,128)(2,1)} %bitcast.126), channel_id=1, replica_groups=mesh['blk'=16,'ulysses'=64] {'ulysses'}, dimensions={0} | all-to-all | bytes 2097152 | tf_op jit(solution)/shard_map/all_to_all | solution.py:29
  82.3 8.1 %all-to-all-start = ((bf16[64,64,128]{2,1,0:T(8,128)(2,1)}), bf16[64,64,128]{2,1,0:T(8,128)(2,1)}, u32[]{:S(2)}, u32[]{:S(2)}) async-start(bf16[64,64,128]{2,1,0:T(8,128)(2,1)} %bitcast.2), calls=%async_computation | async-start | bytes 2097152 | tf_op jit(solution)/shard_map/all_to_all | solution.py:28
  91.3 52.9 %all_gather.6 = bf16[1,2048,128]{2,1,0:T(8,128)(2,1)S(1)} all-gather(bf16[1,128,128]{2,1,0:T(8,128)(2,1)S(1)} %constant_dynamic-slice_fusion.3), channel_id=1, replica_groups=mesh['blk'=16,'ulysses'=64] {'blk'}, dimensions={1}, use_global_device_ids=true | all-gather | bytes 557056 | tf_op jit(solution)/shard_map/all_gather | solution.py:37
  145.3 35.1 %all_gather.7 = bf16[1,2048,128]{2,1,0:T(8,128)(2,1)S(1)} all-gather(bf16[1,128,128]{2,1,0:T(8,128)(2,1)S(1)} %constant_dynamic-slice_fusion.1), channel_id=1, replica_groups=mesh['blk'=16,'ulysses'=64] {'blk'}, dimensions={1}, use_global_device_ids=true | all-gather | bytes 557056 | tf_op jit(solution)/shard_map/all_gather | solution.py:38
  182.0 35.9 %while.20 = (s32[]{:T(128)}, bf16[1,4096,128]{2,1,0:T(8,128)(2,1)}, f32[1,384,128]{2,1,0:T(8,128)S(1)}, f32[1,384,128]{2,1,0:T(8,128)}, s32[1,1]{1,0:T(1,128)}, ...) while((s32[]{:T(128)}, bf16[1,4096,128]{2,1,0:T(8,128)(2,1)}, ...), condition=%wide.region_4.5_spmd.clone, body=%wide.region_0.4_spmd.clone.sunk | while | flops 611717248 | bytes 22454080 | solution.py:116
  182.3 1.3 select_reduce_fusion.2
  188.3 1.6 fusion.79
  191.3 1.3 select_reduce_fusion.2
  197.3 1.6 fusion.79
  200.3 1.3 select_reduce_fusion.2
  206.2 1.6 fusion.79
  215.2 1.6 fusion.79
  219.0 6.7 %broadcast_multiply_fusion = (f32[1,2048,128]{2,0,1:T(1,128)}, f32[1,2048,128]{2,0,1:T(1,128)}) fusion(f32[1,2048,128]{2,0,1:T(1,128)S(1)} %bitcast.124, f32[2048]{0:T(1024)S(1)} %mul.159, f32[1,2048,128]{2,0,1:T(1,128)S(1)} %bitcast.123), kind=kLoop, calls=%fused_computation.57 | loop fusion | flops 524288 | bytes 4202496 | tf_op jit(solution)/shard_map/mul | solution.py:125
  226.5 142.7 %reduce-scatter.3.cloned.1.call-done = f32[1,128,128]{2,0,1:T(1,128)} async-done(((f32[1,2048,128]{2,0,1:T(1,128)}), f32[1,128,128]{2,0,1:T(1,128)}) %reduce-scatter.3.cloned.1.call-update) | async-done | bytes 65552 | tf_op jit(solution)/shard_map/reduce_scatter | solution.py:129
  369.2 114.6 %reduce-scatter.5.cloned.1.call-done = f32[1,128,128]{2,0,1:T(1,128)} async-done(((f32[1,2048,128]{2,0,1:T(1,128)}), f32[1,128,128]{2,0,1:T(1,128)}) %reduce-scatter.5.cloned.1.call-update) | async-done | bytes 65552 | tf_op jit(solution)/shard_map/reduce_scatter | solution.py:130
  485.4 8.6 %all-to-all-start.3 = ((bf16[64,2,128]{2,1,0:T(2,128)(2,1)}), bf16[64,2,128]{2,1,0:T(2,128)(2,1)S(1)}, u32[]{:S(2)}, u32[]{:S(2)}) async-start(bf16[64,2,128]{2,1,0:T(2,128)(2,1)} %bitcast.88), calls=%async_computation.4 | async-start | bytes 65536 | tf_op jit(solution)/shard_map/all_to_all | solution.py:136
  494.7 13.9 %all-to-all-done.3 = bf16[64,2,128]{2,1,0:T(2,128)(2,1)S(1)} async-done(((bf16[64,2,128]{2,1,0:T(2,128)(2,1)}), bf16[64,2,128]{2,1,0:T(2,128)(2,1)S(1)}, u32[]{:S(2)}, u32[]{:S(2)}) %all-to-all-start.3) | async-done | bytes 32800 | tf_op jit(solution)/shard_map/all_to_all | solution.py:136
  508.5 4.8 all-to-all-start.4
  513.3 3.2 copy.53
  517.0 23.4 %reduce.20 = bf16[4096,128]{1,0:T(8,128)(2,1)} reduce(bf16[4096,1,128]{2,1,0:T(2,128)(2,1)S(1)} %bitcast.121, bf16[]{:T(256)} %broadcast.370), dimensions={1}, to_apply=%bitcast.85.reduce_sub_computation | reduce | bytes 2097154
  540.4 2.2 reshape.406
  542.6 15.5 %all-to-all-start.2 = ((bf16[64,2,4096]{2,1,0:T(2,128)(2,1)}), bf16[64,2,4096]{2,1,0:T(2,128)(2,1)}, u32[]{:S(2)}, u32[]{:S(2)}) async-start(bf16[64,2,4096]{2,1,0:T(2,128)(2,1)} %reshape.406), calls=%async_computation.2 | async-start | bytes 2097152 | tf_op jit(solution)/shard_map/all_to_all | solution.py:135
  559.6 48.6 %all-to-all-done.2 = bf16[64,2,4096]{2,1,0:T(2,128)(2,1)} async-done(((bf16[64,2,4096]{2,1,0:T(2,128)(2,1)}), bf16[64,2,4096]{2,1,0:T(2,128)(2,1)}, u32[]{:S(2)}, u32[]{:S(2)}) %all-to-all-start.2) | async-done | bytes 1048608 | tf_op jit(solution)/shard_map/all_to_all | solution.py:135
  608.2 6.5 %reshape.407 = bf16[4096,1,128]{2,1,0:T(2,128)(2,1)S(1)} reshape(bf16[64,2,4096]{2,1,0:T(2,128)(2,1)} %all-to-all-done.2) | data formatting | bytes 2097152
  (122 shorter events, 35.8 us)
Async XLA Ops:
  7.2 84.1 %copy-start = (bf16[32,128,128]{2,1,0:T(8,128)(2,1)S(1)}, bf16[32,128,128]{2,1,0:T(8,128)(2,1)}, u32[]{:S(2)}) copy-start(bf16[32,128,128]{2,1,0:T(8,128)(2,1)} %param.9) | copy-start | bytes 3145732
  82.3 98.6 %all-to-all-start = ((bf16[64,64,128]{2,1,0:T(8,128)(2,1)}), bf16[64,64,128]{2,1,0:T(8,128)(2,1)}, u32[]{:S(2)}, u32[]{:S(2)}) async-start(bf16[64,64,128]{2,1,0:T(8,128)(2,1)} %bitcast.2), calls=%async_computation | async-start | bytes 2097152 | tf_op jit(solution)/shard_map/all_to_all | solution.py:28
  90.4 278.7 %reduce-scatter.3.cloned.1.call-start = ((), (), s32[]{:S(2)}) async-start(), calls=%async_computation.7 | async-start | bytes 1114112 | tf_op jit(solution)/shard_map/reduce_scatter | solution.py:129
  186.3 0.9 copy-start.1
  186.3 3.6 copy-start.2
  190.3 0.7 copy-start.3
  195.2 0.9 copy-start.1
  195.2 3.6 copy-start.2
  199.3 0.7 copy-start.3
  204.2 0.9 copy-start.1
  204.2 3.6 copy-start.2
  208.3 0.7 copy-start.3
  213.2 0.9 copy-start.1
  213.2 3.6 copy-start.2
  217.2 0.7 copy-start.3
  225.7 258.0 %reduce-scatter.5.cloned.1.call-start = ((), (), s32[]{:S(2)}) async-start(), calls=%async_computation.8 | async-start | bytes 1114112 | tf_op jit(solution)/shard_map/reduce_scatter | solution.py:130
  485.4 23.2 %all-to-all-start.3 = ((bf16[64,2,128]{2,1,0:T(2,128)(2,1)}), bf16[64,2,128]{2,1,0:T(2,128)(2,1)S(1)}, u32[]{:S(2)}, u32[]{:S(2)}) async-start(bf16[64,2,128]{2,1,0:T(2,128)(2,1)} %bitcast.88), calls=%async_computation.4 | async-start | bytes 65536 | tf_op jit(solution)/shard_map/all_to_all | solution.py:136
  508.5 34.0 %all-to-all-start.4 = ((bf16[64,2,128]{2,1,0:T(2,128)(2,1)}), bf16[64,2,128]{2,1,0:T(2,128)(2,1)S(1)}, u32[]{:S(2)}, u32[]{:S(2)}) async-start(bf16[64,2,128]{2,1,0:T(2,128)(2,1)} %bitcast.89), calls=%async_computation.6 | async-start | bytes 65536 | tf_op jit(solution)/shard_map/all_to_all | solution.py:137
  542.6 65.7 %all-to-all-start.2 = ((bf16[64,2,4096]{2,1,0:T(2,128)(2,1)}), bf16[64,2,4096]{2,1,0:T(2,128)(2,1)}, u32[]{:S(2)}, u32[]{:S(2)}) async-start(bf16[64,2,4096]{2,1,0:T(2,128)(2,1)} %reshape.406), calls=%async_computation.2 | async-start | bytes 2097152 | tf_op jit(solution)/shard_map/all_to_all | solution.py:135
Sparse Core Ops, SparseCore 0:
  225.9 143.2 reduce-scatter.2
  376.0 107.6 reduce-scatter.4
where the time goes:
time: 624 us; the launch traced here: 623 us
  waiting for transfers between devices  320 us (51%)
  blocking collectives  163 us (26%)
  starting transfers between devices  37.1 us (6%)
  other arithmetic  35.9 us (6%)
  local copies, waits for them, and re-layouts  30.1 us (5%)
  matrix products  21.2 us (3%)
  between operations  14.3 us (2%)
    reduce_scatter x1, waiting for transfers between devices, body(): lax.psum_scatter(spread_keys, 'blk', scatter_dimension=1, tiled=True)  143 us
    reduce_scatter x1, waiting for transfers between devices, body(): lax.psum_scatter(spread_values, 'blk', scatter_dimension=1, tiled=True)  115 us
    all_to_all x1, blocking collectives, body(): lax.all_to_all(packed_grad, 'ulysses', split_axis=0, concat_axis=1, tiled...  75.1 us
    all_gather x1, blocking collectives, body(): lax.all_gather(own_keys, 'blk', axis=1, tiled=True)  52.9 us
    all_to_all x1, waiting for transfers between devices, body(): lax.all_to_all(query_out, 'ulysses', split_axis=1, concat_axis=0, tiled=T...  48.6 us
    all_gather x1, blocking collectives, body(): lax.all_gather(own_values, 'blk', axis=1, tiled=True)  35.1 us
    unnamed x3, other arithmetic  23.4 us
    all_to_all x1, starting transfers between devices, body(): lax.all_to_all(query_out, 'ulysses', split_axis=1, concat_axis=0, tiled=T...  15.5 us
  transfers between devices with their start and end apart: 6, of which 4 were waited for; matrix products, arithmetic and copies ran while one was open for 5% of the time, Pallas kernels for 0%

commit v1 on v0

v1 whole, which is shorter than its diff:
```python
import functools
import math

import jax
import jax.numpy as jnp
from jax import lax
from jax.experimental import pallas as pl
from jax.experimental.pallas import tpu as pltpu
from jax.sharding import PartitionSpec as P

KB = 16
MESH = pl.DeviceIdType.MESH
VMEM_LIMIT = 60 * 1024 * 1024


class Sizes:
    def __init__(self, heads, group_keys, head_dim, tokens, groups, ranks):
        self.heads, self.group_keys, self.dim, self.tokens = heads, group_keys, head_dim, tokens
        self.groups, self.ranks = groups, ranks
        self.half = groups // 2
        self.ny = group_keys // KB
        self.nz = ranks // self.ny
        self.part = heads // self.ny
        self.each = KB // self.nz
        self.units = 2 * self.part // self.nz
        self.major = self.ny // 2
        self.minor = self.ny - 1 - self.major
        self.own_rows = self.ny * self.each
        self.cross_rows = self.half * self.each
        self.stride = tokens * ranks // group_keys
        self.scale = 1.0 / math.sqrt(head_dim)


def where_am_i(sz):
    g = lax.axis_index("blk")
    r = lax.axis_index("ulysses")
    return g, r, g // sz.half, r // sz.nz, r % sz.nz


def greet(sz, g, r, y, z, whole_rows):
    barrier = pltpu.get_barrier_semaphore()
    count = 0
    for d in range(1, sz.groups):
        pl.semaphore_signal(
            barrier, inc=1, device_id=((g + d) % sz.groups, r), device_id_type=MESH
        )
        count += 1
    y_steps = range(1, sz.ny) if whole_rows else sorted({1, sz.ny - 1})
    for d in y_steps:
        pl.semaphore_signal(
            barrier,
            inc=1,
            device_id=(g, (y + d) % sz.ny * sz.nz + z),
            device_id_type=MESH,
        )
        count += 1
    for d in range(1, sz.nz):
        pl.semaphore_signal(
            barrier, inc=1, device_id=(g, y * sz.nz + (z + d) % sz.nz), device_id_type=MESH
        )
        count += 1
    pl.semaphore_wait(barrier, count)


def gather_kernel(
    sz,
    routes_ref,
    k_ref,
    v_ref,
    ft_ref,
    same_buf,
    cross_buf,
    same_send,
    same_recv,
    cross_send,
    cross_recv,
    z_send,
    z_recv,
    y_send,
    y_recv,
):
    g, r, zh, y, z = where_am_i(sz)
    gl = g - zh * sz.half
    half, ny, nz, part = sz.half, sz.ny, sz.nz, sz.part

    for jl in range(half):

        @pl.when(jl >= gl)
        def _(jl=jl):
            ft_ref[:, :, zh * half + jl] = jnp.zeros(
                (sz.heads, 2, KB, sz.dim), ft_ref.dtype
            )

    greet(sz, g, r, y, z, False)

    def cross_copy(i, q):
        u = z * sz.units + q
        return pltpu.make_async_remote_copy(
            src_ref=cross_buf.at[i, q],
            dst_ref=ft_ref.at[y * part + u // 2, u % 2, g],
            send_sem=cross_send.at[i, q],
            recv_sem=cross_recv.at[gl, q],
            device_id=(half + i, r),
            device_id_type=MESH,
        )

    def picker(count, target):
        shape = (count * KB, sz.group_keys)
        row = lax.broadcasted_iota(jnp.int32, shape, 0)
        col = lax.broadcasted_iota(jnp.int32, shape, 1)
        begin = jnp.zeros(shape, jnp.int32)
        for i in range(count):
            chosen = routes_ref[target(i) % sz.groups, g] * KB
            begin = jnp.where(row // KB == i, chosen, begin)
        return (col == begin + row % KB).astype(jnp.bfloat16)

    @pl.when(zh == 0)
    def _():
        pick = picker(half, lambda i: half + i)
        for q in range(sz.units):
            u = z * sz.units + q
            h = y * part + u // 2
            is_key = (u % 2 == 0).astype(jnp.float32)
            chosen = dot(pick, k_ref[h], 1, 0) * is_key + dot(pick, v_ref[h], 1, 0) * (1.0 - is_key)
            cross_buf[:, q] = chosen.astype(cross_buf.dtype).reshape(half, KB, sz.dim)
            for i in range(half):
                cross_copy(i, q).start()

    def same_copy(d):
        return pltpu.make_async_remote_copy(
            src_ref=same_buf.at[d - 1],
            dst_ref=ft_ref.at[:, :, g],
            send_sem=same_send.at[d - 1],
            recv_sem=same_recv.at[gl],
            device_id=(g + d, r),
            device_id_type=MESH,
        )

    if half > 1:
        pick_same = picker(half - 1, lambda i: g + 1 + i)

        def pick_head(h, _):
            for t, ref in ((0, k_ref), (1, v_ref)):
                chosen = dot(pick_same, ref[h], 1, 0).astype(same_buf.dtype)
                same_buf[:, h, t] = chosen.reshape(half - 1, KB, sz.dim)
            return 0

        lax.fori_loop(0, sz.heads, pick_head, 0)
    for d in range(1, half):

        @pl.when(gl + d < half)
        def _(d=d):
            same_copy(d).start()

    @pl.when(zh == 1)
    def _():
        def z_copy(d, q):
            u = z * sz.units + q
            piece = ft_ref.at[y * part + u // 2, u % 2, pl.ds(0, half)]
            return pltpu.make_async_remote_copy(
                src_ref=piece,
                dst_ref=piece,
                send_sem=z_send.at[d - 1, q],
                recv_sem=z_recv.at[z, q],
                device_id=(g, y * nz + (z + d) % nz),
                device_id_type=MESH,
            )

        def z_wait(d, q):
            src = (z + d) % nz
            u = src * sz.units + q
            piece = ft_ref.at[y * part + u // 2, u % 2, pl.ds(0, half)]
            pltpu.make_async_remote_copy(
                src_ref=piece,
                dst_ref=piece,
                send_sem=z_send.at[d - 1, q],
                recv_sem=z_recv.at[src, q],
                device_id=(g, y * nz + src),
                device_id_type=MESH,
            ).wait_recv()

        for q in range(sz.units):
            u = z * sz.units + q
            for i in range(half):
                dst = ft_ref.at[y * part + u // 2, u % 2, i]
                pltpu.make_async_remote_copy(
                    src_ref=dst,
                    dst_ref=dst,
                    send_sem=cross_send.at[i, q],
                    recv_sem=cross_recv.at[i, q],
                    device_id=(i, r),
                    device_id_type=MESH,
                ).wait_recv()
            for d in range(1, nz):
                z_copy(d, q).start()
        for q in range(sz.units):
            for d in range(1, nz):
                z_wait(d, q)

        def y_copy(p, slot, origin, sign):
            piece = ft_ref.at[origin % ny * part + p, :, pl.ds(0, half)]
            return pltpu.make_async_remote_copy(
                src_ref=piece,
                dst_ref=piece,
                send_sem=y_send.at[p, slot],
                recv_sem=y_recv.at[p, slot],
                device_id=(g, (y + sign + ny) % ny * nz + z),
                device_id_type=MESH,
            )

        for s in range(sz.major):

            def step(p, _, s=s):
                sign = 1 - 2 * (p % 2)
                if s > 0:
                    y_copy(p, s - 1, y - s * sign + ny, sign).wait_recv()
                y_copy(p, s, y - s * sign + ny, sign).start()
                if s < sz.minor:
                    if s > 0:
                        y_copy(p, sz.major + s - 1, y + s * sign + ny, sign).wait_recv()
                    y_copy(p, sz.major + s, y + s * sign + ny, -sign).start()
                return 0

            lax.fori_loop(0, part, step, 0)

        def last(p, _):
            sign = 1 - 2 * (p % 2)
            y_copy(p, sz.major - 1, y - sz.major * sign + ny, sign).wait_recv()
            if sz.minor > 0:
                y_copy(p, sz.major + sz.minor - 1, y + sz.minor * sign + ny, sign).wait_recv()
            for s in range(sz.major):
                y_copy(p, s, y - s * sign + ny, sign).wait_send()
            for s in range(sz.minor):
                y_copy(p, sz.major + s, y + s * sign + ny, -sign).wait_send()
            return 0

        lax.fori_loop(0, part, last, 0)
        for q in range(sz.units):
            for d in range(1, nz):
                z_copy(d, q).wait_send()

    @pl.when(zh == 0)
    def _():
        for i in range(half):
            for q in range(sz.units):
                cross_copy(i, q).wait_send()

    for d in range(1, half):

        @pl.when(gl + d < half)
        def _(d=d):
            same_copy(d).wait_send()

    for jl in range(half):

        @pl.when(jl < gl)
        def _(jl=jl):
            dst = ft_ref.at[:, :, zh * half + jl]
            pltpu.make_async_remote_copy(
                src_ref=dst,
                dst_ref=dst,
                send_sem=same_send.at[0],
                recv_sem=same_recv.at[jl],
                device_id=(zh * half + jl, r),
                device_id_type=MESH,
            ).wait_recv()


def gather_far(sz, routes, keys, values):
    vmem = pl.BlockSpec(memory_space=pltpu.VMEM)
    dma = pltpu.SemaphoreType.DMA
    return pl.pallas_call(
        functools.partial(gather_kernel, sz),
        out_shape=jax.ShapeDtypeStruct(
            (sz.heads, 2, sz.groups, KB, sz.dim), jnp.bfloat16
        ),
        in_specs=[pl.BlockSpec(memory_space=pltpu.SMEM), vmem, vmem],
        out_specs=vmem,
        scratch_shapes=[
            pltpu.VMEM((max(1, sz.half - 1), sz.heads, 2, KB, sz.dim), jnp.bfloat16),
            pltpu.VMEM((sz.half, sz.units, KB, sz.dim), jnp.bfloat16),
            dma((max(1, sz.half - 1),)),
            dma((sz.half,)),
            dma((sz.half, sz.units)),
            dma((sz.half, sz.units)),
            dma((max(1, sz.nz - 1), sz.units)),
            dma((sz.nz, sz.units)),
            dma((sz.part, sz.ny)),
            dma((sz.part, sz.ny)),
        ],
        compiler_params=pltpu.CompilerParams(
            collective_id=0, has_side_effects=True, vmem_limit_bytes=VMEM_LIMIT
        ),
        name="gather_far",
    )(routes, keys, values)


def order_matrix(blocks, each):
    count = blocks * KB
    row = lax.broadcasted_iota(jnp.int32, (count, count), 0)
    col = lax.broadcasted_iota(jnp.int32, (count, count), 1)
    rank = row // (blocks * each)
    block = row // each % blocks
    return (col == block * KB + rank * each + row % each).astype(jnp.bfloat16)


def dot(a, b, ca, cb):
    return lax.dot_general(a, b, (((ca,), (cb,)), ((), ())), preferred_element_type=jnp.float32)


def attend_kernel(sz, step_heads, q_ref, og_ref, k_ref, v_ref, ft_ref, dq_ref, px_ref, pc_ref, po_ref):
    g, r, zh, y, z = where_am_i(sz)
    gl = g - zh * sz.half
    half, ny, nz, each, dim = sz.half, sz.ny, sz.nz, sz.each, sz.dim
    n_own, n_far = sz.group_keys, half * KB
    own_order = order_matrix(ny, each)
    far_order = own_order if half == ny else order_matrix(half, each)
    row = lax.broadcasted_iota(jnp.int32, (n_own, sz.tokens), 0)
    tok = r * sz.tokens + lax.broadcasted_iota(jnp.int32, (n_own, sz.tokens), 1)
    key = row // each % ny * KB + row // (ny * each) * each + row % each
    far_row = lax.broadcasted_iota(jnp.int32, (n_far, sz.tokens), 0)
    visible = jnp.concatenate(
        [
            key * sz.stride <= tok,
            jnp.broadcast_to(zh == 1, (n_far, sz.tokens)),
            far_row // KB < gl,
        ],
        axis=0,
    )

    def one_head(i, _):
        q = q_ref[i]
        og = og_ref[i]

        def near(own_ref, t):
            own = dot(own_order, own_ref[i], 1, 0).astype(jnp.bfloat16)
            cross = ft_ref[i, t, pl.ds(0, half)].reshape(n_far, dim)
            cross = dot(far_order, cross, 1, 0).astype(jnp.bfloat16)
            same = ft_ref[i, t, pl.ds(zh * half, half)].reshape(n_far, dim)
            return jnp.concatenate([own, cross, same], axis=0)

        keys = near(k_ref, 0)
        values = near(v_ref, 1)
        scores = dot(keys, q, 1, 1) * sz.scale
        scores = jnp.where(visible, scores, -jnp.inf)
        e = jnp.exp(scores - jnp.max(scores, axis=0, keepdims=True))
        w = e / jnp.sum(e, axis=0, keepdims=True)
        wh = w.astype(jnp.bfloat16)
        dw = dot(values, og, 1, 1)
        delta = jnp.sum(wh.astype(jnp.float32) * dw, axis=0, keepdims=True)
        ds = (w * (dw - delta)).astype(jnp.bfloat16)
        dq_ref[i] = (dot(ds, keys, 0, 0) * sz.scale).astype(dq_ref.dtype)
        dk = dot(ds, q, 1, 0) * sz.scale
        dv = dot(wh, og, 1, 0)
        for t, part in ((0, dk), (1, dv)):
            po_ref[i, t] = part[:n_own].reshape(nz, sz.own_rows, dim)
            pc_ref[i, t] = part[n_own : n_own + n_far].astype(jnp.bfloat16).reshape(
                nz, sz.cross_rows, dim
            )
            px_ref[i, t] = part[n_own + n_far :].astype(jnp.bfloat16).reshape(half, KB, dim)
        return 0

    lax.fori_loop(0, step_heads, one_head, 0)


def attend(sz, query, grad, keys, values, far):
    step_heads = min(8, sz.heads)

    def spec(*dims):
        return pl.BlockSpec((step_heads,) + dims, lambda i: (i,) + (0,) * len(dims))

    shapes = [
        ((sz.tokens, sz.dim), jnp.bfloat16),
        ((2, sz.half, KB, sz.dim), jnp.bfloat16),
        ((2, sz.nz, sz.cross_rows, sz.dim), jnp.bfloat16),
        ((2, sz.nz, sz.own_rows, sz.dim), jnp.float32),
    ]
    return pl.pallas_call(
        functools.partial(attend_kernel, sz, step_heads),
        grid=(sz.heads // step_heads,),
        out_shape=[jax.ShapeDtypeStruct((sz.heads,) + s, d) for s, d in shapes],
        in_specs=[
            spec(sz.tokens, sz.dim),
            spec(sz.tokens, sz.dim),
            spec(sz.group_keys, sz.dim),
            spec(sz.group_keys, sz.dim),
            spec(2, sz.groups, KB, sz.dim),
        ],
        out_specs=[spec(*s) for s, _ in shapes],
        compiler_params=pltpu.CompilerParams(vmem_limit_bytes=VMEM_LIMIT),
        name="attend",
    )(query, grad, keys, values, far)


def reduce_kernel(
    sz,
    routes_ref,
    px_ref,
    pc_ref,
    po_ref,
    kg_ref,
    vg_ref,
    rx,
    ring_c,
    ring_o,
    out_c,
    out_o,
    tot,
    zs_c,
    zs_o,
    zr_c,
    zr_o,
    fin,
    xs,
    xr,
    os_,
    x_send,
    x_recv,
    y_send,
    y_recv,
    z_send,
    z_recv,
    c_send,
    c_recv,
    f_send,
    f_recv,
):
    g, r, zh, y, z = where_am_i(sz)
    gl = g - zh * sz.half
    half, ny, nz, part, each, dim = sz.half, sz.ny, sz.nz, sz.part, sz.each, sz.dim
    own_rows, cross_rows, heads = sz.own_rows, sz.cross_rows, sz.heads
    f32, bf16 = jnp.float32, jnp.bfloat16

    for i in range(half):

        @pl.when(i <= gl)
        def _(i=i):
            rx[:, :, i] = jnp.zeros((heads, 2, KB, dim), bf16)

    greet(sz, g, r, y, z, True)

    def x_copy(jl):
        return pltpu.make_async_remote_copy(
            src_ref=px_ref.at[:, :, jl],
            dst_ref=rx.at[:, :, gl],
            send_sem=x_send.at[jl],
            recv_sem=x_recv.at[gl],
            device_id=(zh * half + jl, r),
            device_id_type=MESH,
        )

    for jl in range(half - 1):

        @pl.when(jl < gl)
        def _(jl=jl):
            x_copy(jl).start()

    mix_shape = (sz.group_keys, half * KB)
    row = lax.broadcasted_iota(jnp.int32, mix_shape, 0)
    col = lax.broadcasted_iota(jnp.int32, mix_shape, 1)
    fits = (row // (ny * each) == col // each % nz) & (row % each == col % each)
    block = row // each % ny
    mix = jnp.zeros(mix_shape, f32)
    for i in range(half):
        chosen = fits & (col // KB == i) & (block == routes_ref[zh * half + i, g])
        mix = jnp.where(chosen, 1.0, mix)
    mix = mix.astype(bf16)

    def own_part(h, t):
        more = dot(mix, rx[h, t].reshape(half * KB, dim), 1, 0)
        return po_ref[h, t] + more.reshape(nz, own_rows, dim)

    def cross_part(h, t):
        return pc_ref[h, t].astype(f32)

    kinds = (
        (0, cross_part, ring_c, out_c, zs_c, zr_c, cross_rows),
        (1, own_part, ring_o, out_o, zs_o, zr_o, own_rows),
    )

    def y_copy(kind, p, slot, sign):
        return pltpu.make_async_remote_copy(
            src_ref=kind[3].at[p, slot],
            dst_ref=kind[2].at[p, slot],
            send_sem=y_send.at[kind[0], p, slot],
            recv_sem=y_recv.at[kind[0], p, slot],
            device_id=(g, (y + sign + ny) % ny * nz + z),
            device_id_type=MESH,
        )

    def z_copy(kind, p, d):
        to = (z + d) % nz
        return pltpu.make_async_remote_copy(
            src_ref=kind[4].at[p, to],
            dst_ref=kind[5].at[p, z],
            send_sem=z_send.at[kind[0], p, d],
            recv_sem=z_recv.at[kind[0], p, z],
            device_id=(g, y * nz + to),
            device_id_type=MESH,
        )

    def z_wait(kind, p, d):
        src = (z + d) % nz
        pltpu.make_async_remote_copy(
            src_ref=kind[4].at[p, src],
            dst_ref=kind[5].at[p, src],
            send_sem=z_send.at[kind[0], p, d],
            recv_sem=z_recv.at[kind[0], p, src],
            device_id=(g, y * nz + src),
            device_id_type=MESH,
        ).wait_recv()

    def ring_step(kind, s):
        _, mine, ring, out, zs, _, rows = kind

        def one(p, _):
            sign = 1 - 2 * (p % 2)
            ways = []
            if s < sz.major:
                ways.append((0, sign, y + (sz.major - s) * sign))
            if s < sz.minor:
                ways.append((sz.major, -sign, y - (sz.minor - s) * sign))
            for base, way, chunk in ways:
                h = (chunk + ny) % ny * part + p
                if s > 0:
                    y_copy(kind, p, base + s - 1, way).wait_recv()
                for t in range(2):
                    total = mine(h, t)
                    if s > 0:
                        total = total + ring[p, base + s - 1, t].astype(f32)
                    out[p, base + s, t] = total.astype(bf16)
                y_copy(kind, p, base + s, way).start()
            if s == sz.major:
                y_copy(kind, p, sz.major - 1, sign).wait_recv()
                if sz.minor > 0:
                    y_copy(kind, p, sz.major + sz.minor - 1, -sign).wait_recv()
                for t in range(2):
                    total = mine(y * part + p, t) + ring[p, sz.major - 1, t].astype(f32)
                    if sz.minor > 0:
                        total = total + ring[p, sz.major + sz.minor - 1, t].astype(f32)
                    zs[p, :, t] = total.astype(bf16)
                    tot[kind[0], p, t, :, pl.ds(0, rows)] = total
                for d in range(1, nz):
                    z_copy(kind, p, d).start()
            return 0

        lax.fori_loop(0, part, one, 0)

    def finish(kind, store):
        zr, rows = kind[5], kind[6]

        def one(p, _):
            for d in range(1, nz):
                z_wait(kind, p, d)
            for t in range(2):
                total = tot[kind[0], p, t, z, pl.ds(0, rows)]
                for d in range(1, nz):
                    total = total + zr[p, (z + d) % nz, t].astype(f32)
                fin[kind[0], t, pl.ds(0, rows)] = total
                store(p, t)
            return 0

        lax.fori_loop(0, part, one, 0)

    def c_copy(j):
        return pltpu.make_async_remote_copy(
            src_ref=xs.at[j],
            dst_ref=xr.at[gl],
            send_sem=c_send.at[j],
            recv_sem=c_recv.at[gl],
            device_id=(j, r),
            device_id_type=MESH,
        )

    def cross_step(s):
        @pl.when(zh == 1)
        def _():
            ring_step(kinds[0], s)

    cross_step(0)

    for i in range(1, half):

        @pl.when(i > gl)
        def _(i=i):
            pltpu.make_async_remote_copy(
                src_ref=px_ref.at[:, :, 0],
                dst_ref=rx.at[:, :, i],
                send_sem=x_send.at[0],
                recv_sem=x_recv.at[i],
                device_id=(zh * half + i, r),
                device_id_type=MESH,
            ).wait_recv()

    ring_step(kinds[1], 0)
    for s in range(1, sz.major + 1):
        cross_step(s)
        ring_step(kinds[1], s)

    @pl.when(zh == 1)
    def _():
        def store(p, t):
            for j in range(half):
                xs[j, t, p] = fin[0, t, pl.ds(j * each, each)]

        finish(kinds[0], store)
        for j in range(half):
            c_copy(j).start()

    def store_own(p, t):
        for b in range(ny):
            os_[b, t, p] = fin[1, t, pl.ds(b * each, each)]

    finish(kinds[1], store_own)

    @pl.when(zh == 0)
    def _():
        for i in range(half):
            pltpu.make_async_remote_copy(
                src_ref=xs.at[0],
                dst_ref=xr.at[i],
                send_sem=c_send.at[0],
                recv_sem=c_recv.at[i],
                device_id=(half + i, r),
                device_id_type=MESH,
            ).wait_recv()
        for b in range(ny):
            total = os_[b]
            for i in range(half):
                total = total + jnp.where(routes_ref[half + i, g] == b, xr[i], 0.0)
            os_[b] = total

    def f_copy(t, d):
        to = (y + d) % ny
        return pltpu.make_async_remote_copy(
            src_ref=os_.at[to, t],
            dst_ref=(kg_ref, vg_ref)[t].at[pl.ds(y * part, part)],
            send_sem=f_send.at[t, d],
            recv_sem=f_recv.at[t, y],
            device_id=(g, to * nz + z),
            device_id_type=MESH,
        )

    for d in range(1, ny):
        for t in range(2):
            f_copy(t, d).start()
    for t, ref in ((0, kg_ref), (1, vg_ref)):
        ref[pl.ds(y * part, part)] = os_[y, t]

    def sends(kind):
        def one(p, _):
            sign = 1 - 2 * (p % 2)
            for slot in range(ny - 1):
                y_copy(kind, p, slot, sign).wait_send()
            for d in range(1, nz):
                z_copy(kind, p, d).wait_send()
            return 0

        lax.fori_loop(0, part, one, 0)

    @pl.when(zh == 1)
    def _():
        sends(kinds[0])
        for j in range(half):
            c_copy(j).wait_send()

    sends(kinds[1])
    for jl in range(half - 1):

        @pl.when(jl < gl)
        def _(jl=jl):
            x_copy(jl).wait_send()

    for d in range(1, ny):
        src = (y + d) % ny
        for t in range(2):
            f_copy(t, d).wait_send()
            dst = (kg_ref, vg_ref)[t].at[pl.ds(src * part, part)]
            pltpu.make_async_remote_copy(
                src_ref=dst,
                dst_ref=dst,
                send_sem=f_send.at[t, d],
                recv_sem=f_recv.at[t, src],
                device_id=(g, src * nz + z),
                device_id_type=MESH,
            ).wait_recv()


def reduce_parts(sz, routes, px, pc, po):
    vmem = pl.BlockSpec(memory_space=pltpu.VMEM)
    dma = pltpu.SemaphoreType.DMA
    f32, bf16 = jnp.float32, jnp.bfloat16
    heads, half, ny, nz, part, each, dim = (
        sz.heads,
        sz.half,
        sz.ny,
        sz.nz,
        sz.part,
        sz.each,
        sz.dim,
    )
    own_rows, cross_rows = sz.own_rows, sz.cross_rows
    most = max(own_rows, cross_rows)
    out = jax.ShapeDtypeStruct((heads, each, dim), f32)
    return pl.pallas_call(
        functools.partial(reduce_kernel, sz),
        out_shape=[out, out],
        in_specs=[pl.BlockSpec(memory_space=pltpu.SMEM), vmem, vmem, vmem],
        out_specs=[vmem, vmem],
        scratch_shapes=[
            pltpu.VMEM((heads, 2, half, KB, dim), bf16),
            pltpu.VMEM((part, ny - 1, 2, nz, cross_rows, dim), bf16),
            pltpu.VMEM((part, ny - 1, 2, nz, own_rows, dim), bf16),
            pltpu.VMEM((part, ny - 1, 2, nz, cross_rows, dim), bf16),
            pltpu.VMEM((part, ny - 1, 2, nz, own_rows, dim), bf16),
            pltpu.VMEM((2, part, 2, nz, most, dim), f32),
            pltpu.VMEM((part, nz, 2, cross_rows, dim), bf16),
            pltpu.VMEM((part, nz, 2, own_rows, dim), bf16),
            pltpu.VMEM((part, nz, 2, cross_rows, dim), bf16),
            pltpu.VMEM((part, nz, 2, own_rows, dim), bf16),
            pltpu.VMEM((2, 2, most, dim), f32),
            pltpu.VMEM((half, 2, part, each, dim), f32),
            pltpu.VMEM((half, 2, part, each, dim), f32),
            pltpu.VMEM((ny, 2, part, each, dim), f32),
            dma((half,)),
            dma((half,)),
            dma((2, part, ny - 1)),
            dma((2, part, ny - 1)),
            dma((2, part, nz)),
            dma((2, part, nz)),
            dma((half,)),
            dma((half,)),
            dma((2, ny)),
            dma((2, ny)),
        ],
        compiler_params=pltpu.CompilerParams(
            collective_id=1, has_side_effects=True, vmem_limit_bytes=VMEM_LIMIT
        ),
        name="reduce_parts",
    )(routes, px, pc, po)


def solution(mesh):
    def body(query_rows, out_grad, key_rows, value_rows, routes):
        heads, tokens, dim = query_rows.shape
        sz = Sizes(
            heads, key_rows.shape[1], dim, tokens, mesh.shape["blk"], mesh.shape["ulysses"]
        )
        far = gather_far(sz, routes, key_rows, value_rows)
        query_grad, px, pc, po = attend(sz, query_rows, out_grad, key_rows, value_rows, far)
        key_grad, value_grad = reduce_parts(sz, routes, px, pc, po)
        return query_grad, key_grad, value_grad

    return jax.shard_map(
        body,
        mesh=mesh,
        in_specs=(
            P(None, ("blk", "ulysses"), None),
            P(None, ("blk", "ulysses"), None),
            P(None, "blk", None),
            P(None, "blk", None),
            P(),
        ),
        out_specs=(
            P(None, ("blk", "ulysses"), None),
            P(None, ("blk", "ulysses"), None),
            P(None, ("blk", "ulysses"), None),
        ),
        check_vma=False,
    )
```

time: 624 us -> 202 us (0.32)
  the two profiles are of different devices: /device:TPU:2 before, /device:TPU:128 now
where the time goes in v1:
time: 202 us
  Pallas kernels  198 us (98%)
  local copies, waits for them, and re-layouts  2.75 us (1%)
    pallas_call x1, Pallas kernels, reduce_parts(): pl.pallas_call(functools.partial(reduce_kernel, sz), out_shape=[out, out]...  119 us
    pallas_call x1, Pallas kernels, gather_far(): pl.pallas_call(functools.partial(gather_kernel, sz), out_shape=jax.ShapeD...  52.2 us
    pallas_call x1, Pallas kernels, attend(): pl.pallas_call(functools.partial(attend_kernel, sz, step_heads), grid=(sz...  26.8 us

profile of v1, /device:TPU:128, one launch (start us, length us, event | category | flops | bytes accessed | tf_op | source)
XLA Modules:
  0.0 201.5 jit_solution(2218609838746264141)
XLA Ops:
  0.6 52.2 %gather_far.1.ft_ref = bf16[32,2,16,16,128]{4,3,2,1,0:T(8,128)(2,1)} custom-call(s32[16,16]{1,0:T(8,128)} %routes_ref.3, bf16[32,128,128]{2,1,0:T(8,128)(2,1)} %k_ref.3, bf16[32,128,128]{2,1,0:T(8,128)(2,1)} %v_ref.3), custom_call_target="tpu_custom_call" | custom-call | tf_op jit(solution)/shard_map/gather_far/pallas_call | solution.py:272
  52.8 26.8 %attend.1 = (bf16[32,128,128]{2,1,0:T(8,128)(2,1)}, bf16[32,2,8,16,128]{4,3,2,1,0:T(8,128)(2,1)}, bf16[32,2,8,16,128]{4,3,2,1,0:T(8,128)(2,1)}, f32[32,2,8,16,128]{4,3,2,1,0:T(8,128)}) custom-call(bf16[32,128,128]{2,1,0:T(8,128)(2,1)} %q_ref.1, bf16[32,128,128]{2,1,0:T(8,128)(2,1)} %og_ref.1, bf16[32,128,128]{2,1,0:T(8,128)(2,1)} %k_ref.3, ...), custom_call_target="tpu_custom_call" | custom-call | tf_op jit(solution)/shard_map/attend/pallas_call | solution.py:378
  79.6 119.1 %reduce_parts.1 = (f32[32,2,128]{2,1,0:T(2,128)}, f32[32,2,128]{2,1,0:T(2,128)}) custom-call(s32[16,16]{1,0:T(8,128)} %routes_ref.3, bf16[32,2,8,16,128]{4,3,2,1,0:T(8,128)(2,1)} %get-tuple-element.10.px_ref, bf16[32,2,8,16,128]{4,3,2,1,0:T(8,128)(2,1)} %get-tuple-element.11.pc_ref, f32[32,2,8,16,128]{4,3,2,1,0:T(8,128)} %get-tuple-element.12.po_ref), custom_call_target="tpu_custom_call" | custom-call | tf_op jit(solution)/shard_map/reduce_parts/pallas_call | solution.py:705
  198.8 1.4 copy.10
  200.1 1.4 copy.11

commit v2 on v0

v2 whole, which is shorter than its diff:
```python
import functools
import math

import jax
import jax.numpy as jnp
from jax import lax
from jax.experimental import pallas as pl
from jax.experimental.pallas import tpu as pltpu
from jax.sharding import PartitionSpec as P

KB = 16
MESH = pl.DeviceIdType.MESH
VMEM_LIMIT = 60 * 1024 * 1024


class Sizes:
    def __init__(self, heads, group_keys, head_dim, tokens, groups, ranks):
        self.heads, self.group_keys, self.dim, self.tokens = heads, group_keys, head_dim, tokens
        self.groups, self.ranks = groups, ranks
        self.half = groups // 2
        self.ny = group_keys // KB
        self.nz = ranks // self.ny
        self.part = heads // self.ny
        self.each = KB // self.nz
        self.units = 2 * self.part // self.nz
        self.major = self.ny // 2
        self.minor = self.ny - 1 - self.major
        self.own_rows = self.ny * self.each
        self.stride = tokens * ranks // group_keys
        self.scale = 1.0 / math.sqrt(head_dim)


def where_am_i(sz):
    g = lax.axis_index("blk")
    r = lax.axis_index("ulysses")
    return g, r, g // sz.half, r // sz.nz, r % sz.nz


def greet(sz, g, r, zh, y, z):
    barrier = pltpu.get_barrier_semaphore()

    def signal(group, rank):
        pl.semaphore_signal(barrier, inc=1, device_id=(group, rank), device_id_type=MESH)

    for d in range(1, sz.groups):
        signal((g + d) % sz.groups, r)
    for d in range(1, sz.ny):
        signal(g, (y + d) % sz.ny * sz.nz + z)
    for d in range(1, sz.nz):
        signal(g, y * sz.nz + (z + d) % sz.nz)
    for i in range(sz.half):
        signal(zh * z + (1 - zh) * (sz.half + i), y * sz.nz + zh * i + (1 - zh) * g)
    pl.semaphore_wait(barrier, sz.groups + sz.ny + sz.nz + sz.half - 3)


def order_matrix(blocks, each):
    count = blocks * KB
    row = lax.broadcasted_iota(jnp.int32, (count, count), 0)
    col = lax.broadcasted_iota(jnp.int32, (count, count), 1)
    rank = row // (blocks * each)
    block = row // each % blocks
    return (col == block * KB + rank * each + row % each).astype(jnp.bfloat16)


def dot(a, b, ca, cb):
    return lax.dot_general(a, b, (((ca,), (cb,)), ((), ())), preferred_element_type=jnp.float32)


def kernel(
    sz,
    routes_ref,
    q_ref,
    og_ref,
    k_ref,
    v_ref,
    dq_ref,
    kg_ref,
    vg_ref,
    same_buf,
    cross_buf,
    fs,
    fc,
    kp,
    vp,
    bias,
    mix,
    px,
    pc,
    po,
    rx,
    ring_c,
    ring_o,
    out_c,
    out_o,
    tot,
    zs,
    zr,
    fin,
    xs,
    xr,
    os_,
    same_send,
    same_recv,
    cross_send,
    cross_recv,
    gz_send,
    gz_recv,
    gy_send,
    gy_recv,
    x_send,
    x_recv,
    y_send,
    y_recv,
    z_send,
    z_recv,
    c_send,
    c_recv,
    f_send,
    f_recv,
):
    g, r, zh, y, z = where_am_i(sz)
    gl = g - zh * sz.half
    half, ny, nz, part, each, dim = sz.half, sz.ny, sz.nz, sz.part, sz.each, sz.dim
    heads, major, minor, own_rows = sz.heads, sz.major, sz.minor, sz.own_rows
    n_own, n_far = sz.group_keys, half * KB
    f32, bf16 = jnp.float32, jnp.bfloat16

    def remote(src, dst, send_sem, recv_sem, group, rank):
        return pltpu.make_async_remote_copy(
            src_ref=src,
            dst_ref=dst,
            send_sem=send_sem,
            recv_sem=recv_sem,
            device_id=(group, rank),
            device_id_type=MESH,
        )

    greet(sz, g, r, zh, y, z)


    def cross_copy(i, n):
        u = z * sz.units + n
        return remote(
            cross_buf.at[i, n],
            fc.at[u // 2, y, u % 2, g],
            cross_send.at[i, n],
            cross_recv.at[gl, n],
            half + i,
            r,
        )

    def picker(count, target):
        shape = (count * KB, n_own)
        row = lax.broadcasted_iota(jnp.int32, shape, 0)
        col = lax.broadcasted_iota(jnp.int32, shape, 1)
        begin = jnp.zeros(shape, jnp.int32)
        for i in range(count):
            chosen = routes_ref[target(i) % sz.groups, g] * KB
            begin = jnp.where(row // KB == i, chosen, begin)
        return (col == begin + row % KB).astype(bf16)

    @pl.when(zh == 0)
    def _():
        pick = picker(half, lambda i: half + i)
        for n in range(sz.units):
            u = z * sz.units + n
            h = y * part + u // 2
            is_key = (u % 2 == 0).astype(f32)
            chosen = dot(pick, k_ref[h], 1, 0) * is_key + dot(pick, v_ref[h], 1, 0) * (1.0 - is_key)
            cross_buf[:, n] = chosen.astype(bf16).reshape(half, KB, dim)
            for i in range(half):
                cross_copy(i, n).start()

    def same_copy(p, d):
        return remote(
            same_buf.at[d - 1, p],
            fs.at[p, gl],
            same_send.at[p, d - 1],
            same_recv.at[p, gl],
            g + d,
            r,
        )

    if half > 1:
        pick_same = picker(half - 1, lambda i: g + 1 + i)

        def pick_part(p, _):
            def pick_head(c, _):
                for t, ref in ((0, k_ref), (1, v_ref)):
                    chosen = dot(pick_same, ref[c * part + p], 1, 0).astype(bf16)
                    same_buf[:, p, c, t] = chosen.reshape(half - 1, KB, dim)
                return 0

            lax.fori_loop(0, ny, pick_head, 0)
            for d in range(1, half):

                @pl.when(gl + d < half)
                def _(d=d):
                    same_copy(p, d).start()

            return 0

        lax.fori_loop(0, part, pick_part, 0)

    def gz_copy(d, n):
        u = z * sz.units + n
        piece = fc.at[u // 2, y, u % 2]
        return remote(
            piece,
            piece,
            gz_send.at[d - 1, n],
            gz_recv.at[z, n],
            g,
            y * nz + (z + d) % nz,
        )

    def gz_wait(d, n):
        src = (z + d) % nz
        u = src * sz.units + n
        piece = fc.at[u // 2, y, u % 2]
        remote(
            piece, piece, gz_send.at[d - 1, n], gz_recv.at[src, n], g, y * nz + src
        ).wait_recv()

    @pl.when(zh == 1)
    def _():
        for n in range(sz.units):
            u = z * sz.units + n
            for i in range(half):
                dst = fc.at[u // 2, y, u % 2, i]
                remote(dst, dst, cross_send.at[i, n], cross_recv.at[i, n], i, r).wait_recv()
            for d in range(1, nz):
                gz_copy(d, n).start()


    nothing = jnp.zeros((part, ny, 2, KB, dim), bf16)
    for i in range(half):

        @pl.when(i >= gl)
        def _(i=i):
            fs[:, i] = nothing

        @pl.when(i <= gl)
        def _(i=i):
            rx[:, i] = nothing

    @pl.when(zh == 0)
    def _():
        fc[...] = jnp.zeros((part, ny, 2, half, KB, dim), bf16)

    row = lax.broadcasted_iota(jnp.int32, (n_own, sz.tokens), 0)
    tok = r * sz.tokens + lax.broadcasted_iota(jnp.int32, (n_own, sz.tokens), 1)
    key = row // each % ny * KB + row // (ny * each) * each + row % each
    far_row = lax.broadcasted_iota(jnp.int32, (n_far, sz.tokens), 0)
    bias[pl.ds(0, n_own)] = jnp.where(key * sz.stride <= tok, 0.0, -jnp.inf)
    bias[pl.ds(n_own, n_far)] = jnp.where(far_row >= (1 - zh) * n_far, 0.0, -jnp.inf)
    bias[pl.ds(n_own + n_far, n_far)] = jnp.where(far_row // KB < gl, 0.0, -jnp.inf)

    mix_shape = (n_own, n_far)
    row = lax.broadcasted_iota(jnp.int32, mix_shape, 0)
    col = lax.broadcasted_iota(jnp.int32, mix_shape, 1)
    fits = (row // (ny * each) == col // each % nz) & (row % each == col % each)
    block = row // each % ny
    spots = jnp.zeros(mix_shape, f32)
    for i in range(half):
        chosen = fits & (col // KB == i) & (block == routes_ref[zh * half + i, g])
        spots = jnp.where(chosen, 1.0, spots)
    mix[...] = spots.astype(bf16)

    own_order = order_matrix(ny, each)

    def order_own(h, _):
        kp[h] = dot(own_order, k_ref[h], 1, 0).astype(bf16)
        vp[h] = dot(own_order, v_ref[h], 1, 0).astype(bf16)
        return 0

    lax.fori_loop(0, heads, order_own, 0)


    def gy_copy(p, slot, origin, way):
        piece = fc.at[p, (origin + ny) % ny]
        return remote(
            piece,
            piece,
            gy_send.at[p, slot],
            gy_recv.at[p, slot],
            g,
            (y + way + ny) % ny * nz + z,
        )

    @pl.when(zh == 1)
    def _():
        for n in range(sz.units):
            for d in range(1, nz):
                gz_wait(d, n)

        for s in range(major):

            def step(p, _, s=s):
                sign = 1 - 2 * (p % 2)
                if s > 0:
                    gy_copy(p, s - 1, y - s * sign, sign).wait_recv()
                gy_copy(p, s, y - s * sign, sign).start()
                if s < minor:
                    if s > 0:
                        gy_copy(p, major + s - 1, y + s * sign, -sign).wait_recv()
                    gy_copy(p, major + s, y + s * sign, -sign).start()
                return 0

            lax.fori_loop(0, part, step, 0)

    def far_is_here(p):
        sign = 1 - 2 * (p % 2)

        @pl.when(zh == 1)
        def _():
            gy_copy(p, major - 1, y - major * sign, sign).wait_recv()
            if minor > 0:
                gy_copy(p, major + minor - 1, y + minor * sign, -sign).wait_recv()

        for i in range(half - 1):

            @pl.when(i < gl)
            def _(i=i):
                dst = fs.at[p, i]
                remote(
                    dst, dst, same_send.at[p, 0], same_recv.at[p, i], zh * half + i, r
                ).wait_recv()


    log2e = math.log2(math.e)

    def attend(p, chunks):
        qs = [q_ref[c * part + p] for c in chunks]
        ogs = [og_ref[c * part + p] for c in chunks]

        def near(own, c, t):
            cross = fc[p, c, t].reshape(n_far, dim)
            same = fs[p, :, c, t].reshape(n_far, dim)
            return jnp.concatenate([own[c * part + p], cross, same], axis=0)

        keys = [near(kp, c, 0) for c in chunks]
        values = [near(vp, c, 1) for c in chunks]
        scores = [dot(k, q, 1, 1) * (sz.scale * log2e) + bias[...] for k, q in zip(keys, qs)]
        dws = [dot(v, og, 1, 1) for v, og in zip(values, ogs)]
        es = [jnp.exp2(x - jnp.max(x, axis=0, keepdims=True)) for x in scores]
        ws = [e * (1.0 / jnp.sum(e, axis=0, keepdims=True)) for e in es]
        whs = [w.astype(bf16) for w in ws]
        deltas = [
            jnp.sum(wh.astype(f32) * dw, axis=0, keepdims=True) for wh, dw in zip(whs, dws)
        ]
        dss = [
            (w * (dw - delta)).astype(bf16) for w, dw, delta in zip(ws, dws, deltas)
        ]
        for c, q, og, k, ds, wh in zip(chunks, qs, ogs, keys, dss, whs):
            dq_ref[c * part + p] = (dot(ds, k, 0, 0) * sz.scale).astype(dq_ref.dtype)
            dk = dot(ds, q, 1, 0) * sz.scale
            dv = dot(wh, og, 1, 0)
            for t, grad in ((0, dk), (1, dv)):
                po[p, c, t] = grad[:n_own].reshape(nz, own_rows, dim)
                pc[p, c, t] = grad[n_own : n_own + n_far].astype(bf16).reshape(half, KB, dim)
                px[p, :, c, t] = grad[n_own + n_far :].astype(bf16).reshape(half, KB, dim)


    def x_copy(p, jl):
        return remote(
            px.at[p, jl],
            rx.at[p, gl],
            x_send.at[p, jl],
            x_recv.at[p, gl],
            zh * half + jl,
            r,
        )

    def own_part(p, c, t):
        more = dot(mix[...], rx[p, :, c, t].reshape(n_far, dim), 1, 0)
        return po[p, c, t] + more.reshape(nz, own_rows, dim)

    def cross_part(p, c, t):
        return pc[p, c, t].astype(f32)

    cross = (0, cross_part, ring_c, out_c)
    own = (1, own_part, ring_o, out_o)

    def y_copy(kind, p, slot, way):
        return remote(
            kind[3].at[p, slot],
            kind[2].at[p, slot],
            y_send.at[kind[0], p, slot],
            y_recv.at[kind[0], p, slot],
            g,
            (y + way + ny) % ny * nz + z,
        )

    def ring_step(kind, p, s):
        sign = 1 - 2 * (p % 2)

        def hop(base, way, c):
            c = (c + ny) % ny

            @pl.when(s == 0)
            def _():
                for t in range(2):
                    kind[3][p, base, t] = kind[1](p, c, t).astype(bf16)

            @pl.when(s > 0)
            def _():
                y_copy(kind, p, base + s - 1, way).wait_recv()
                for t in range(2):
                    total = kind[1](p, c, t) + kind[2][p, base + s - 1, t].astype(f32)
                    kind[3][p, base + s, t] = total.astype(bf16)

            y_copy(kind, p, base + s, way).start()

        hop(0, sign, y + (major - s) * sign)
        if minor > 0:

            @pl.when(s < minor)
            def _():
                hop(major, -sign, y - (minor - s) * sign)

    def z_copy(kind, p, d):
        to = (z + d) % nz
        return remote(
            zs.at[kind[0], p, to],
            zr.at[kind[0], p, z],
            z_send.at[kind[0], p, d],
            z_recv.at[kind[0], p, z],
            g,
            y * nz + to,
        )

    def ring_end(kind, p):
        sign = 1 - 2 * (p % 2)
        ring = kind[2]
        y_copy(kind, p, major - 1, sign).wait_recv()
        if minor > 0:
            y_copy(kind, p, major + minor - 1, -sign).wait_recv()
        for t in range(2):
            total = kind[1](p, y, t) + ring[p, major - 1, t].astype(f32)
            if minor > 0:
                total = total + ring[p, major + minor - 1, t].astype(f32)
            zs[kind[0], p, :, t] = total.astype(bf16)
            tot[kind[0], p, t] = total
        for d in range(1, nz):
            z_copy(kind, p, d).start()

    def finish(kind, p, store):
        for d in range(1, nz):
            src = (z + d) % nz
            remote(
                zs.at[kind[0], p, src],
                zr.at[kind[0], p, src],
                z_send.at[kind[0], p, d],
                z_recv.at[kind[0], p, src],
                g,
                y * nz + src,
            ).wait_recv()
        for t in range(2):
            total = tot[kind[0], p, t, z]
            for d in range(1, nz):
                total = total + zr[kind[0], p, (z + d) % nz, t].astype(f32)
            fin[kind[0], t] = total
            store(p, t)

    def store_cross(p, t):
        for c in range(nz):
            xs[c, t, p] = fin[0, t, pl.ds(c * each, each)]

    def store_own(p, t):
        for b in range(ny):
            os_[b, t, p] = fin[1, t, pl.ds(b * each, each)]

    def c_copy(c):
        return remote(xs.at[c], xr.at[gl], c_send.at[c], c_recv.at[gl], z, y * nz + c)

    late = min(2, major - 1)

    def turn(it, _):
        p = it // major
        s = it % major
        sign = 1 - 2 * (p % 2)

        @pl.when(p < part)
        def _():
            @pl.when(s == 0)
            def _():
                far_is_here(p)

            attend(
                p,
                [
                    (y + (major - s) * sign + ny) % ny,
                    (y - (minor - s) * sign + ny) % ny,
                ],
            )

            @pl.when(s == major - 1)
            def _():
                for jl in range(half - 1):

                    @pl.when(jl < gl)
                    def _(jl=jl):
                        x_copy(p, jl).start()

            @pl.when(zh == 1)
            def _():
                ring_step(cross, p, s)

        @pl.when(p >= 1)
        def _():
            @pl.when((s == 0) & (zh == 1))
            def _():
                ring_end(cross, p - 1)

            @pl.when(s == 0)
            def _():
                for i in range(1, half):

                    @pl.when(i > gl)
                    def _(i=i):
                        dst = rx.at[p - 1, i]
                        remote(
                            dst, dst, x_send.at[p - 1, 0], x_recv.at[p - 1, i], zh * half + i, r
                        ).wait_recv()

            ring_step(own, p - 1, s)

            @pl.when((s == late) & (zh == 1))
            def _():
                finish(cross, p - 1, store_cross)

                @pl.when(p == part)
                def _():
                    for c in range(nz):
                        c_copy(c).start()

        @pl.when(p >= 2)
        def _():
            @pl.when(s == 0)
            def _():
                ring_end(own, p - 2)

            @pl.when(s == late)
            def _():
                finish(own, p - 2, store_own)

        return 0

    lax.fori_loop(0, (part + 1) * major, turn, 0)
    ring_end(own, part - 1)
    finish(own, part - 1, store_own)

    @pl.when(zh == 0)
    def _():
        for i in range(half):
            remote(
                xs.at[0], xr.at[i], c_send.at[0], c_recv.at[i], half + i, y * nz + g
            ).wait_recv()
        for b in range(ny):
            total = os_[b]
            for i in range(half):
                total = total + jnp.where(routes_ref[half + i, g] == b, xr[i], 0.0)
            os_[b] = total

    def f_copy(t, d):
        to = (y + d) % ny
        return remote(
            os_.at[to, t],
            (kg_ref, vg_ref)[t].at[pl.ds(y * part, part)],
            f_send.at[t, d],
            f_recv.at[t, y],
            g,
            to * nz + z,
        )

    for d in range(1, ny):
        for t in range(2):
            f_copy(t, d).start()
    for t, ref in ((0, kg_ref), (1, vg_ref)):
        ref[pl.ds(y * part, part)] = os_[y, t]


    def sends(kind):
        def one(p, _):
            sign = 1 - 2 * (p % 2)
            for slot in range(ny - 1):
                y_copy(kind, p, slot, sign).wait_send()
            for d in range(1, nz):
                z_copy(kind, p, d).wait_send()
            return 0

        lax.fori_loop(0, part, one, 0)

    @pl.when(zh == 0)
    def _():
        for i in range(half):
            for n in range(sz.units):
                cross_copy(i, n).wait_send()

    @pl.when(zh == 1)
    def _():
        def ring_left(p, _):
            for slot in range(ny - 1):
                gy_copy(p, slot, y, 1).wait_send()
            return 0

        lax.fori_loop(0, part, ring_left, 0)
        for n in range(sz.units):
            for d in range(1, nz):
                gz_copy(d, n).wait_send()
        sends(cross)
        for c in range(nz):
            c_copy(c).wait_send()

    sends(own)

    def straight(p, _):
        for d in range(1, half):

            @pl.when(gl + d < half)
            def _(d=d):
                same_copy(p, d).wait_send()

        for jl in range(half - 1):

            @pl.when(jl < gl)
            def _(jl=jl):
                x_copy(p, jl).wait_send()

        return 0

    lax.fori_loop(0, part, straight, 0)

    for d in range(1, ny):
        src = (y + d) % ny
        for t in range(2):
            f_copy(t, d).wait_send()
            dst = (kg_ref, vg_ref)[t].at[pl.ds(src * part, part)]
            remote(
                dst, dst, f_send.at[t, d], f_recv.at[t, src], g, src * nz + z
            ).wait_recv()


def backward(sz, routes, query, grad, keys, values):
    vmem = pl.BlockSpec(memory_space=pltpu.VMEM)
    dma = pltpu.SemaphoreType.DMA
    f32, bf16 = jnp.float32, jnp.bfloat16
    heads, half, ny, nz, part, each, dim, own_rows = (
        sz.heads,
        sz.half,
        sz.ny,
        sz.nz,
        sz.part,
        sz.each,
        sz.dim,
        sz.own_rows,
    )
    near = sz.group_keys + 2 * half * KB
    small = jax.ShapeDtypeStruct((heads, each, dim), f32)
    ring_c = pltpu.VMEM((part, ny - 1, 2, half, KB, dim), bf16)
    ring_o = pltpu.VMEM((part, ny - 1, 2, nz, own_rows, dim), bf16)
    return pl.pallas_call(
        functools.partial(kernel, sz),
        out_shape=[jax.ShapeDtypeStruct((heads, sz.tokens, dim), bf16), small, small],
        in_specs=[pl.BlockSpec(memory_space=pltpu.SMEM), vmem, vmem, vmem, vmem],
        out_specs=[vmem, vmem, vmem],
        scratch_shapes=[
            pltpu.VMEM((max(1, half - 1), part, ny, 2, KB, dim), bf16),
            pltpu.VMEM((half, sz.units, KB, dim), bf16),
            pltpu.VMEM((part, half, ny, 2, KB, dim), bf16),
            pltpu.VMEM((part, ny, 2, half, KB, dim), bf16),
            pltpu.VMEM((heads, sz.group_keys, dim), bf16),
            pltpu.VMEM((heads, sz.group_keys, dim), bf16),
            pltpu.VMEM((near, sz.tokens), f32),
            pltpu.VMEM((sz.group_keys, half * KB), bf16),
            pltpu.VMEM((part, half, ny, 2, KB, dim), bf16),
            pltpu.VMEM((part, ny, 2, half, KB, dim), bf16),
            pltpu.VMEM((part, ny, 2, nz, own_rows, dim), f32),
            pltpu.VMEM((part, half, ny, 2, KB, dim), bf16),
            ring_c,
            ring_o,
            ring_c,
            ring_o,
            pltpu.VMEM((2, part, 2, nz, KB, dim), f32),
            pltpu.VMEM((2, part, nz, 2, KB, dim), bf16),
            pltpu.VMEM((2, part, nz, 2, KB, dim), bf16),
            pltpu.VMEM((2, 2, KB, dim), f32),
            pltpu.VMEM((nz, 2, part, each, dim), f32),
            pltpu.VMEM((half, 2, part, each, dim), f32),
            pltpu.VMEM((ny, 2, part, each, dim), f32),
            dma((part, max(1, half - 1))),
            dma((part, half)),
            dma((half, sz.units)),
            dma((half, sz.units)),
            dma((max(1, nz - 1), sz.units)),
            dma((nz, sz.units)),
            dma((part, ny)),
            dma((part, ny)),
            dma((part, half)),
            dma((part, half)),
            dma((2, part, ny - 1)),
            dma((2, part, ny - 1)),
            dma((2, part, nz)),
            dma((2, part, nz)),
            dma((nz,)),
            dma((half,)),
            dma((2, ny)),
            dma((2, ny)),
        ],
        compiler_params=pltpu.CompilerParams(
            collective_id=0, has_side_effects=True, vmem_limit_bytes=VMEM_LIMIT
        ),
        name="backward",
    )(routes, query, grad, keys, values)


def solution(mesh):
    def body(query_rows, out_grad, key_rows, value_rows, routes):
        heads, tokens, dim = query_rows.shape
        sz = Sizes(
            heads, key_rows.shape[1], dim, tokens, mesh.shape["blk"], mesh.shape["ulysses"]
        )
        assert sz.half == sz.nz and sz.own_rows == KB
        return backward(sz, routes, query_rows, out_grad, key_rows, value_rows)

    return jax.shard_map(
        body,
        mesh=mesh,
        in_specs=(
            P(None, ("blk", "ulysses"), None),
            P(None, ("blk", "ulysses"), None),
            P(None, "blk", None),
            P(None, "blk", None),
            P(),
        ),
        out_specs=(
            P(None, ("blk", "ulysses"), None),
            P(None, ("blk", "ulysses"), None),
            P(None, ("blk", "ulysses"), None),
        ),
        check_vma=False,
    )
```

time: 624 us -> 165 us (0.26)
  the two profiles are of different devices: /device:TPU:2 before, /device:TPU:64 now
where the time goes in v2:
time: 165 us; the launch traced here: 164 us
  Pallas kernels  160 us (97%)
  local copies, waits for them, and re-layouts  3.7 us (2%)
    pallas_call x1, Pallas kernels, backward(): pl.pallas_call(functools.partial(kernel, sz), out_shape=[jax.ShapeDtypeSt...  160 us
    unnamed x7, local copies, waits for them, and re-layouts  3.7 us

profile of v2, /device:TPU:64, one launch (start us, length us, event | category | flops | bytes accessed | tf_op | source)
XLA Modules:
  0.0 164.3 jit_solution(16745621167617601073)
XLA Ops:
  0.6 159.9 %backward.1 = (bf16[32,128,128]{2,1,0:T(8,128)(2,1)}, f32[32,2,128]{2,1,0:T(2,128)}, f32[32,2,128]{2,1,0:T(2,128)}) custom-call(s32[16,16]{1,0:T(8,128)} %routes_ref.1, bf16[32,128,128]{2,1,0:T(8,128)(2,1)} %q_ref.1, bf16[32,128,128]{2,1,0:T(8,128)(2,1)} %og_ref.1, bf16[32,128,128]{2,1,0:T(8,128)(2,1)} %k_ref.1, bf16[32,128,128]{2,1,0:T(8,128)(2,1)} %v_ref.1), custom_call_target="tpu_custom_call" | custom-call | tf_op jit(solution)/shard_map/backward/pallas_call | solution.py:663
  160.6 0.0 copy-start.1
  160.6 2.3 %copy.11 = bf16[32,128,128]{2,1,0:T(8,128)(2,1)} copy(bf16[32,128,128]{2,1,0:T(8,128)(2,1)} %get-tuple-element.6) | data formatting | bytes 2097152
  162.9 0.0 copy-done.1
  162.9 0.0 copy-start
  162.9 0.6 copy.12
  163.5 0.2 copy-done
  163.7 0.6 copy.13
Async XLA Ops:
  160.6 2.3 %copy-start.1 = (f32[32,2,128]{2,1,0:T(2,128)S(1)}, f32[32,2,128]{2,1,0:T(2,128)}, u32[]{:S(2)}) copy-start(f32[32,2,128]{2,1,0:T(2,128)} %get-tuple-element.7) | copy-start | bytes 98308
  162.9 0.8 copy-start
